TPU v7x, 32 devices: a whole 2x2x4 slice. The times are simulated.
32 devices in a mesh: rep: 16 (over z, y, core), shard: 2 (over x).
Axes of the slice: x: 2, y: 2, z: 4, core: 2. Of those that a mesh axis runs over, the one named last changes fastest.
Arguments:
- grad_xproj: bfloat16 [64, 2, 3072, 128], P(('rep', 'shard')), may hold values from -32 to 32
- grad_chan: bfloat16 [64, 2, 118, 3072], P(('rep', 'shard')), may hold values from -32 to 32
- grad_embed: bfloat16 [64, 1024, 1536], P(('rep', 'shard')), may hold values from -32 to 32
- weight_xproj: float32 [2, 3072, 128], P(None, 'shard'), may hold values from -0.3125 to 0.3125
- weight_chan: float32 [2, 118, 3072], P(None, None, 'shard'), may hold values from -0.3125 to 0.3125
- weight_embed: float32 [1024, 1536], P('shard'), may hold values from -0.3125 to 0.3125
- moment_xproj: float32 [2, 3072, 128], P(None, 'shard'), may hold values from -0.015625 to 0.015625
- moment_chan: float32 [2, 118, 3072], P(None, None, 'shard'), may hold values from -0.015625 to 0.015625
- moment_embed: float32 [1024, 1536], P('shard'), may hold values from -0.015625 to 0.015625
- second_xproj: float32 [2, 3072, 128], P(None, 'shard'), may hold values from 1e-08 to 1e-05
- second_chan: float32 [2, 118, 3072], P(None, None, 'shard'), may hold values from 1e-08 to 1e-05
- second_embed: float32 [1024, 1536], P('shard'), may hold values from 1e-08 to 1e-05
Outputs:
- new_weight_xproj: float32 [2, 3072, 128], P(None, 'shard')
- new_weight_chan: float32 [2, 118, 3072], P(None, None, 'shard')
- new_weight_embed: float32 [1024, 1536], P('shard')
- new_moment_xproj: float32 [2, 3072, 128], P(None, 'shard')
- new_moment_chan: float32 [2, 118, 3072], P(None, None, 'shard')
- new_moment_embed: float32 [1024, 1536], P('shard')
- new_second_xproj: float32 [2, 3072, 128], P(None, 'shard')
- new_second_chan: float32 [2, 118, 3072], P(None, None, 'shard')
- new_second_embed: float32 [1024, 1536], P('shard')
- full_xproj: bfloat16 [2, 3072, 128], replicated
- full_chan: bfloat16 [2, 118, 3072], replicated
- full_embed: bfloat16 [1024, 1536], replicated
- pre_norm: float32 [1], replicated
All inputs are finite; a program needn't handle non-finite values.
Results may differ from a plain program's by a relative error of at most 0.00085.
Values may be sent and summed in bfloat16 or wider, within the bound.
A program may use at most 448 MiB of HBM per device.

v0:
```python
import jax
import jax.numpy as jnp
from jax import lax
from jax.sharding import PartitionSpec as P

beta_one = 0.9
beta_two = 0.999
learn_rate = 0.003
decay_rate = 0.1
epsilon = 1e-08
correct_one = 0.9999734386011124
correct_two = 0.09520785288629094


def adamw_update(weight, moment, second, gradient, clip_factor):
    clipped = clip_factor * gradient
    new_moment = beta_one * moment + (1.0 - beta_one) * clipped
    new_second = beta_two * second + (1.0 - beta_two) * clipped * clipped
    step_size = new_moment / correct_one / (jnp.sqrt(new_second / correct_two) + epsilon)
    new_weight = weight - learn_rate * (step_size + decay_rate * weight)
    return (new_weight, new_moment, new_second)


def on_device(
    grad_xproj,
    grad_chan,
    grad_embed,
    weight_xproj,
    weight_chan,
    weight_embed,
    moment_xproj,
    moment_chan,
    moment_embed,
    second_xproj,
    second_chan,
    second_embed,
):
    count_rep = lax.axis_size("rep")
    count_shard = lax.axis_size("shard")
    summed_x = jnp.sum(grad_xproj, axis=0, dtype=jnp.float32)
    summed_c = jnp.sum(grad_chan, axis=0, dtype=jnp.float32)
    summed_e = jnp.sum(grad_embed, axis=0, dtype=jnp.float32)
    group = (
        lax.psum_scatter(
            summed_x.astype(jnp.bfloat16), "shard", scatter_dimension=1, tiled=True
        ).astype(jnp.float32),
        lax.psum_scatter(
            summed_c.astype(jnp.bfloat16), "shard", scatter_dimension=2, tiled=True
        ).astype(jnp.float32),
        lax.psum_scatter(
            summed_e.astype(jnp.bfloat16), "shard", scatter_dimension=0, tiled=True
        ).astype(jnp.float32),
    )
    blocks = lax.psum((group[0], group[1], group[2]), "rep")
    inverse = 1.0 / (grad_xproj.shape[0] * count_rep * count_shard)
    mean_x = blocks[0] * inverse
    mean_c = blocks[1] * inverse
    mean_e = blocks[2] * inverse
    partial_squares = jnp.sum(mean_x * mean_x) + jnp.sum(mean_c * mean_c) + jnp.sum(mean_e * mean_e)
    squares = lax.psum(partial_squares, "shard")
    norm_value = jnp.sqrt(squares)
    clip_factor = jnp.minimum(1.0, 1.0 / (norm_value + 1e-06))
    wx, mx, vx = adamw_update(weight_xproj, moment_xproj, second_xproj, mean_x, clip_factor)
    wc, mc, vc = adamw_update(weight_chan, moment_chan, second_chan, mean_c, clip_factor)
    we, me, ve = adamw_update(weight_embed, moment_embed, second_embed, mean_e, clip_factor)
    gathered = (
        lax.all_gather(wx.astype(jnp.bfloat16), "shard", axis=1, tiled=True),
        lax.all_gather(wc.astype(jnp.bfloat16), "shard", axis=2, tiled=True),
        lax.all_gather(we.astype(jnp.bfloat16), "shard", axis=0, tiled=True),
    )
    return (
        wx,
        wc,
        we,
        mx,
        mc,
        me,
        vx,
        vc,
        ve,
        gathered[0],
        gathered[1],
        gathered[2],
        jnp.reshape(norm_value, (1,)),
    )


def solution(mesh):
    placed = (
        P(("rep", "shard"), None, None, None),
        P(("rep", "shard"), None, None, None),
        P(("rep", "shard"), None, None),
        P(None, "shard", None),
        P(None, None, "shard"),
        P("shard", None),
        P(None, "shard", None),
        P(None, None, "shard"),
        P("shard", None),
        P(None, "shard", None),
        P(None, None, "shard"),
        P("shard", None),
    )
    return jax.shard_map(
        on_device,
        mesh=mesh,
        in_specs=placed,
        out_specs=(
            P(None, "shard", None),
            P(None, None, "shard"),
            P("shard", None),
            P(None, "shard", None),
            P(None, None, "shard"),
            P("shard", None),
            P(None, "shard", None),
            P(None, None, "shard"),
            P("shard", None),
            P(),
            P(),
            P(),
            P(),
        ),
        check_vma=False,
    )
```

profile of v0, /device:TPU:1, one launch (start us, length us, event | category | flops | bytes accessed | tf_op | source)
XLA Modules:
  0.0 554.5 jit_solution(16868018088984456349)
XLA Ops:
  7.2 0.0 reduce-scatter.10.cloned.1.call-start
  7.2 6.5 %reduce_sum.65 = bf16[2,118,3072]{2,0,1:T(2,128)(2,1)S(1)} reduce(bf16[2,2,118,3072]{3,1,2,0:T(2,128)(2,1)} %param.13, bf16[]{:T(256)} %constant.14.clone.1), dimensions={0}, to_apply=%region_4.0 | reduce | flops 724992 | bytes 4349954 | tf_op jit(solution)/shard_map/reduce_sum | solution.py:41
  13.7 66.3 %copy.25 = bf16[2,118,3072]{0,1,2:T(8,128)(2,1)} copy(bf16[2,118,3072]{2,0,1:T(2,128)(2,1)S(1)} %reduce_sum.65) | data formatting | bytes 2899968
  80.0 0.0 copy-start.1
  80.0 86.8 %reshape.30 = bf16[3072,236]{1,0:T(8,128)(2,1)} reshape(bf16[3072,118,2]{2,1,0:T(8,128)(2,1)} %bitcast.1) | data formatting | bytes 2899968
  166.8 0.0 reduce-scatter.10.cloned.1.call-update
  166.8 0.0 reduce-scatter.6.cloned.1.call-start
  166.9 0.0 copy-done.1
  166.9 2.2 reduce_sum.63
  169.0 0.0 reduce-scatter.6.cloned.1.call-update
  169.1 0.0 reduce-scatter.8.cloned.1.call-start
  169.1 6.5 %reduce_sum.67 = bf16[1024,1536]{1,0:T(8,128)(2,1)} reduce(bf16[2,1024,1536]{2,1,0:T(8,128)(2,1)} %param.14, bf16[]{:T(256)} %constant.14.clone.1), dimensions={0}, to_apply=%region_8.0 | reduce | flops 1572864 | bytes 9437186 | tf_op jit(solution)/shard_map/reduce_sum | solution.py:42
  175.6 0.0 reduce-scatter.8.cloned.1.call-update
  175.6 0.2 all-gather.6.cloned.1.call-start
  175.9 19.2 %reduce-scatter.10.cloned.1.call-done = bf16[1536,236]{1,0:T(8,128)(2,1)} async-done(((bf16[3072,236]{1,0:T(8,128)(2,1)}), bf16[1536,236]{1,0:T(8,128)(2,1)}) %reduce-scatter.10.cloned.1.call-update) | async-done | bytes 725008
  195.1 37.8 %reshape.31 = bf16[1536,118,2]{2,1,0:T(8,128)(2,1)} reshape(bf16[1536,236]{1,0:T(8,128)(2,1)} %reduce-scatter.10.cloned.1.call-done) | data formatting | bytes 1449984
  232.9 42.1 %copy.26 = bf16[2,118,1536]{2,0,1:T(2,128)(2,1)} copy(bf16[2,118,1536]{0,1,2:T(8,128)(2,1)} %bitcast.4) | data formatting | bytes 1449984
  275.0 0.0 reduce-scatter.6.cloned.1.call-done
  275.0 0.0 reduce-scatter.8.cloned.1.call-done
  275.0 137.6 %all-reduce.2 = (f32[2,1536,128]{2,1,0:T(8,128)}, f32[2,118,1536]{2,0,1:T(2,128)}, f32[512,1536]{1,0:T(8,128)S(1)}) all-reduce(bf16[2,1536,128]{2,1,0:T(8,128)(2,1)} %reduce-scatter.6.cloned.1.call-done, bf16[2,118,1536]{2,0,1:T(2,128)(2,1)} %copy.26, ...), channel_id=1, replica_groups=mesh['rep'=16,'shard'=2] {'rep'}, use_global_device_ids=true, to_apply=%region_2.0 | all-reduce | flops 1542144 | bytes 9252864 | tf_op jit(solution)/shard_map/psum | solution.py:54
  412.6 0.0 copy-start
  412.6 2.5 multiply_reduce_fusion.1
  415.1 0.0 copy-done
  415.1 2.1 multiply_reduce_fusion.2
  417.2 1.4 multiply_reduce_fusion
  420.6 4.3 psum.31
  425.6 8.4 %fusion.5 = (bf16[2,118,1536]{2,0,1:T(2,128)(2,1)}, f32[2,118,1536]{2,0,1:T(2,128)}, f32[2,118,1536]{2,0,1:T(2,128)}, f32[2,118,1536]{2,0,1:T(2,128)}) fusion(f32[2,118,1536]{2,0,1:T(2,128)} %param.16, f32[2,118,1536]{2,0,1:T(2,128)} %get-tuple-element.14, f32[]{:T(128)S(6)} %mul.157, f32[2,118,1536]{2,0,1:T(2,128)} %param.19, f32[2,118,1536]{2,0,1:T(2,128)} %param.22), kind=kLoop, calls=%fused_computation.16 | loop fusion | flops 6162432 | bytes 10874884 | tf_op jit(solution)/shard_map/convert_element_type | solution.py:68
  434.1 0.0 all-gather.6.cloned.1.call-update
  434.1 0.0 all-gather.4.cloned.1.call-start
  434.1 6.1 %fusion.7 = (bf16[2,1536,128]{2,1,0:T(8,128)(2,1)}, f32[2,1536,128]{2,1,0:T(8,128)}, f32[2,1536,128]{2,1,0:T(8,128)}, f32[2,1536,128]{2,1,0:T(8,128)}) fusion(f32[2,1536,128]{2,1,0:T(8,128)} %param.15, f32[2,1536,128]{2,1,0:T(8,128)} %get-tuple-element.13, f32[]{:T(128)S(6)} %mul.157, f32[2,1536,128]{2,1,0:T(8,128)} %param.18, f32[2,1536,128]{2,1,0:T(8,128)} %param.21), kind=kLoop, calls=%fused_computation.17 | loop fusion | flops 6684672 | bytes 11796484 | tf_op jit(solution)/shard_map/convert_element_type | solution.py:67
  440.2 0.0 all-gather.4.cloned.1.call-update
  440.3 0.3 all-gather.8.cloned.1.call-start
  440.5 7.8 %fusion.3 = (bf16[512,1536]{1,0:T(8,128)(2,1)}, f32[512,1536]{1,0:T(8,128)}, f32[512,1536]{1,0:T(8,128)}, f32[512,1536]{1,0:T(8,128)}) fusion(f32[512,1536]{1,0:T(8,128)} %param.17, f32[512,1536]{1,0:T(8,128)S(1)} %get-tuple-element.15, f32[]{:T(128)S(6)} %mul.157, f32[512,1536]{1,0:T(8,128)} %param.20, f32[512,1536]{1,0:T(8,128)} %param.23), kind=kLoop, calls=%fused_computation.15 | loop fusion | flops 13369344 | bytes 23592964 | tf_op jit(solution)/shard_map/convert_element_type | solution.py:69
  448.4 0.0 all-gather.8.cloned.1.call-update
  448.4 13.9 %all-gather.6.cloned.1.call-done = bf16[2,118,3072]{2,0,1:T(2,128)(2,1)} async-done(((bf16[2,118,1536]{2,0,1:T(2,128)(2,1)}), bf16[2,118,3072]{2,0,1:T(2,128)(2,1)}) %all-gather.6.cloned.1.call-update) | async-done | bytes 1450000 | tf_op jit(solution)/shard_map/all_gather | solution.py:68
  462.3 29.3 %all-gather.4.cloned.1.call-done = bf16[2,3072,128]{2,1,0:T(8,128)(2,1)} async-done(((bf16[2,1536,128]{2,1,0:T(8,128)(2,1)}), bf16[2,3072,128]{2,1,0:T(8,128)(2,1)}) %all-gather.4.cloned.1.call-update) | async-done | bytes 1572880 | tf_op jit(solution)/shard_map/all_gather | solution.py:67
  491.6 47.0 %all-gather.8.cloned.1.call-done = bf16[1024,1536]{1,0:T(8,128)(2,1)} async-done(((bf16[512,1536]{1,0:T(8,128)(2,1)}), bf16[1024,1536]{1,0:T(8,128)(2,1)}) %all-gather.8.cloned.1.call-update) | async-done | bytes 3145744 | tf_op jit(solution)/shard_map/all_gather | solution.py:69
  538.6 0.0 copy-start.2
  538.6 2.8 copy.36
  541.4 3.5 copy.37
  544.9 0.0 copy-done.2
  544.9 1.7 copy.38
Async XLA Ops:
  7.2 187.9 %reduce-scatter.10.cloned.1.call-start = ((), (), s32[]{:S(2)}) async-start(), calls=%async_computation.8 | async-start | bytes 2359296
  80.0 86.8 %copy-start.1 = (bf16[2,2,3072,128]{3,2,1,0:T(8,128)(2,1)S(1)}, bf16[2,2,3072,128]{3,2,1,0:T(8,128)(2,1)}, u32[]{:S(2)}) copy-start(bf16[2,2,3072,128]{3,2,1,0:T(8,128)(2,1)} %param.12) | copy-start | bytes 9437188
  166.8 108.2 %reduce-scatter.6.cloned.1.call-start = ((), (), s32[]{:S(2)}) async-start(), calls=%async_computation.3 | async-start | bytes 2359296 | tf_op jit(solution)/shard_map/reduce_scatter | solution.py:44
  169.1 106.0 %reduce-scatter.8.cloned.1.call-start = ((), (), s32[]{:S(2)}) async-start(), calls=%async_computation.4 | async-start | bytes 4718592 | tf_op jit(solution)/shard_map/reduce_scatter | solution.py:50
  175.6 286.6 %all-gather.6.cloned.1.call-start = ((), (), s32[]{:S(2)}) async-start(), calls=%async_computation.6 | async-start | bytes 2174976 | tf_op jit(solution)/shard_map/all_gather | solution.py:68
  412.6 2.5 copy-start
  434.1 57.5 %all-gather.4.cloned.1.call-start = ((), (), s32[]{:S(2)}) async-start(), calls=%async_computation.5 | async-start | bytes 2359296 | tf_op jit(solution)/shard_map/all_gather | solution.py:67
  440.3 98.3 %all-gather.8.cloned.1.call-start = ((), (), s32[]{:S(2)}) async-start(), calls=%async_computation.7 | async-start | bytes 4718592 | tf_op jit(solution)/shard_map/all_gather | solution.py:69
  538.6 6.3 %copy-start.2 = (bf16[1024,1536]{1,0:T(8,128)(2,1)S(1)}, bf16[1024,1536]{1,0:T(8,128)(2,1)}, u32[]{:S(2)}) copy-start(bf16[1024,1536]{1,0:T(8,128)(2,1)} %all-gather.8.cloned.1.call-done) | copy-start | bytes 9437188
Sparse Core Ops, SparseCore 0:
  166.9 28.1 reduce-scatter.9
  198.0 26.0 reduce-scatter.5
  227.0 43.3 reduce-scatter.7
  434.2 28.0 all-gather.5
  464.3 27.2 all-gather.3
  493.6 44.9 all-gather.7
where the time goes:
time: 559 us; the launch traced here: 555 us
  local copies, waits for them, and re-layouts  241 us (43%)
  blocking collectives  142 us (25%)
  waiting for transfers between devices  110 us (20%)
  other arithmetic  43.6 us (8%)
  between operations  18 us (3%)
    unnamed x13, local copies, waits for them, and re-layouts  241 us
    psum x1, blocking collectives, on_device(): blocks = lax.psum((group[0], group[1], group[2]), 'rep')  138 us
    all_gather x1, waiting for transfers between devices, on_device(): lax.all_gather(we.astype(jnp.bfloat16), 'shard', axis=0, tiled=True)  47 us
    all_gather x1, waiting for transfers between devices, on_device(): lax.all_gather(wx.astype(jnp.bfloat16), 'shard', axis=1, tiled=True)  29.3 us
    unnamed x7, waiting for transfers between devices  19.3 us
    all_gather x1, waiting for transfers between devices, on_device(): lax.all_gather(wc.astype(jnp.bfloat16), 'shard', axis=2, tiled=True)  13.9 us
  transfers between devices with their start and end apart: 6, of which 4 were waited for; matrix products, arithmetic and copies ran while one was open for 18% of the time, Pallas kernels for 0%

commit v1 on v0

v1 whole, which is shorter than its diff:
```python
import functools

import jax
import jax.numpy as jnp
from jax import lax
from jax.experimental import pallas as pl
from jax.experimental.pallas import tpu as pltpu
from jax.sharding import PartitionSpec as P

beta_one = 0.9
beta_two = 0.999
learn_rate = 0.003
decay_rate = 0.1
epsilon = 1e-08
correct_one = 0.9999734386011124
correct_two = 0.09520785288629094

F32 = jnp.float32
BF16 = jnp.bfloat16
MESH = pl.DeviceIdType.MESH
VMEM = pl.BlockSpec(memory_space=pltpu.VMEM)
HBM = pl.BlockSpec(memory_space=pl.ANY)
PIECES = ((32, 1536), (192, 128), (64, 384))
TAIL = 54
LIMIT = 52 * 1024 * 1024


def adamw_update(weight, moment, second, gradient, clip_factor):
    clipped = clip_factor * gradient
    new_moment = beta_one * moment + (1.0 - beta_one) * clipped
    new_second = beta_two * second + (1.0 - beta_two) * clipped * clipped
    root = jnp.sqrt(new_second * (1.0 / correct_two)) + epsilon
    step_size = new_moment * (1.0 / correct_one) / root
    new_weight = weight - learn_rate * (step_size + decay_rate * weight)
    return (new_weight, new_moment, new_second)


def sum_embed(g_ref, o_ref):
    o_ref[...] = (g_ref[0].astype(F32) + g_ref[1].astype(F32)).astype(BF16)


def sum_xproj(g_ref, o_ref):
    o_ref[0, 0] = (g_ref[0, 0].astype(F32) + g_ref[1, 0].astype(F32)).astype(BF16)


def sum_chan(g_ref, o_ref):
    for c in range(2):
        rows = 64 if c == 0 else TAIL
        for z in range(4):
            at = (0, slice(c * 64, c * 64 + rows), slice(z * 384, z * 384 + 384))
            total = g_ref[(0, *at)].astype(F32) + g_ref[(1, *at)].astype(F32)
            if rows < 64:
                o_ref[0, c, 0, z] = jnp.zeros((64, 384), BF16)
            o_ref[0, c, 0, z, 0:rows] = total.astype(BF16)


def local_sums(grad_e, grad_x, grad_c):
    e = pl.pallas_call(
        sum_embed,
        grid=(8,),
        in_specs=[pl.BlockSpec((2, 128, 1536), lambda i: (0, i, 0))],
        out_specs=pl.BlockSpec((128, 1536), lambda i: (i, 0)),
        out_shape=jax.ShapeDtypeStruct((1024, 1536), BF16),
        name="sum_embed",
    )(grad_e)
    x = pl.pallas_call(
        sum_xproj,
        grid=(2, 2),
        in_specs=[pl.BlockSpec((2, 1, 1536, 128), lambda s, c: (0, c, s, 0))],
        out_specs=pl.BlockSpec((1, 1, 1536, 128), lambda s, c: (s, c, 0, 0)),
        out_shape=jax.ShapeDtypeStruct((2, 2, 1536, 128), BF16),
        name="sum_xproj",
    )(grad_x)
    c = pl.pallas_call(
        sum_chan,
        grid=(2, 2),
        in_specs=[pl.BlockSpec((2, 1, 118, 1536), lambda s, y: (0, y, 0, s))],
        out_specs=pl.BlockSpec((1, 2, 1, 4, 64, 384), lambda s, y: (s, 0, y, 0, 0, 0)),
        out_shape=jax.ShapeDtypeStruct((2, 2, 2, 4, 64, 384), BF16),
        name="sum_chan",
    )(grad_c)
    return e, x, c


def exchange(reps, inverse, *refs):
    inp = refs[0:3]
    states = refs[3:12]
    grad = refs[12:15]
    other = refs[15:18]
    norm_ref, clip_ref = refs[18:20]
    bc, b2, b3, b4 = refs[20:23], refs[23:26], refs[26:29], refs[29:32]
    piece = refs[32:35]
    held = refs[35:44]
    gpad, sq, sqr, loads, pair_s, pair_r, many_s, many_r = refs[44:52]

    rep, s = lax.axis_index("rep"), lax.axis_index("shard")
    stride_z, stride_y = reps // 4, reps // 8
    c = lax.rem(rep, 2)
    y = lax.rem(rep // stride_y, 2)
    z = rep // stride_z
    sib = (rep + 1 - 2 * c, s)
    ynb = (rep + (1 - 2 * y) * stride_y, s)
    xnb = (rep, 1 - s)
    zs = [lax.rem(z + d, 4) for d in (1, 2, 3)]
    znb = [(rep + (t - z) * stride_z, s) for t in zs]

    barrier = pltpu.get_barrier_semaphore()
    for dev in (sib, ynb, xnb, *znb):
        pl.semaphore_signal(barrier, inc=1, device_id=dev, device_id_type=MESH)
    pl.semaphore_wait(barrier, 6)

    pending = []
    count = [0, 0]

    def pair(src, dst, dev):
        k = count[0]
        count[0] += 1
        copy = pltpu.make_async_remote_copy(
            src_ref=src, dst_ref=dst, send_sem=pair_s.at[k], recv_sem=pair_r.at[k],
            device_id=dev, device_id_type=MESH)
        copy.start()
        pending.append(copy)
        return copy

    def spread(source, slot):
        k = count[1]
        count[1] += 1
        waits = []
        for d, (t, dev) in enumerate(zip(zs, znb)):
            copy = pltpu.make_async_remote_copy(
                src_ref=source(t), dst_ref=slot(z), send_sem=many_s.at[k, d],
                recv_sem=many_r.at[k, z], device_id=dev, device_id_type=MESH)
            copy.start()
            pending.append(copy)
            waits.append(pltpu.make_async_remote_copy(
                src_ref=source(t), dst_ref=slot(t), send_sem=many_s.at[k, d],
                recv_sem=many_r.at[k, t], device_id=dev, device_id_type=MESH))
        return waits

    def add(into, at_into, of, at_of, n):
        def one(k, carry):
            a, b = at_into(k), at_of(k)
            into[a] = (into[a].astype(F32) + of[b].astype(F32)).astype(BF16)
            return carry
        lax.fori_loop(0, n, one, 0)

    first = [pair(inp[i].at[:, 1 - c], bc[i], sib) for i in range(3)]

    place = y * 4 + z
    loading = []
    for k in range(3):
        row = pl.multiple_of((c * 8 + place) * 32, 32)
        loading.append(pltpu.make_async_copy(
            states[k].at[pl.ds(row, 32), :], held[k], loads.at[k]))
        row = pl.multiple_of(place * 192, 192)
        loading.append(pltpu.make_async_copy(
            states[3 + k].at[c, pl.ds(row, 192), :], held[3 + k], loads.at[3 + k]))
        col = pl.multiple_of(z * 384, 384)
        loading.append(pltpu.make_async_copy(
            states[6 + k].at[y, :, pl.ds(col, 384)], held[6 + k], loads.at[6 + k]))
    for copy in loading:
        copy.start()

    second = []
    for i in range(3):
        first[i].wait_recv()
        for half in (0, 1):
            if i == 0:
                keep = s if half else 1 - s
                add(bc[i], lambda k: (keep, k // 4, k % 4),
                    inp[i], lambda k: (keep, c, k // 4, k % 4), 8)
                if not half:
                    second.append(pair(bc[i].at[1 - s], b2[i], xnb))
            else:
                keep = y if half else 1 - y
                add(bc[i], lambda k: (k // 4, keep, k % 4),
                    inp[i], lambda k: (k // 4, c, keep, k % 4), 8)
                if not half:
                    second.append(pair(bc[i].at[:, 1 - y], b2[i], ynb))
    third = []
    for i in range(3):
        second[i].wait_recv()
        mine, dev = (y, ynb) if i == 0 else (s, xnb)
        for half in (0, 1):
            keep = mine if half else 1 - mine
            if i == 0:
                add(b2[i], lambda k: (keep, k), bc[i], lambda k: (s, keep, k), 4)
            else:
                add(b2[i], lambda k: (keep, k), bc[i], lambda k: (keep, y, k), 4)
            if not half:
                third.append(pair(b2[i].at[1 - mine], b3[i], dev))
    fourth = []
    for i in range(3):
        third[i].wait_recv()
        mine = y if i == 0 else s
        add(b3[i], lambda k: (k,), b2[i], lambda k: (mine, k), 4)
        fourth.append(spread(lambda t: b3[i].at[t], lambda t: b4[i].at[t]))

    sq[...] = jnp.zeros((8, 128), F32)
    gpad[...] = jnp.zeros((128, 384), F32)
    wave_g = []
    for i in range(3):
        for wait in fourth[i]:
            wait.wait_recv()
        rows, cols = PIECES[i]
        total = b3[i][z].astype(F32)
        for t in zs:
            total = total + b4[i][t].astype(F32)
        grad[i][c, y, z] = total.astype(BF16)
        mean = total * inverse
        tile = (mean * mean).reshape(rows // 8, 8, cols).sum(axis=0)
        part = sq[...]
        for k in range(cols // 128):
            part = part + tile[:, k * 128:k * 128 + 128]
        sq[...] = part
        wave_g.append(spread(lambda t: grad[i].at[c, y, z], lambda t: grad[i].at[c, y, t]))

    for k, dev in enumerate((sib, xnb, ynb)):
        sqr[k, 0] = sq[...]
        pair(sqr.at[k, 0], sqr.at[k, 1], dev).wait_recv()
        sq[...] = sqr[k, 0] + sqr[k, 1]
    sqr[3, z] = sq[...]
    for wait in spread(lambda t: sqr.at[3, z], lambda t: sqr.at[3, t]):
        wait.wait_recv()
    squares = jnp.sum(sqr[3, 0] + sqr[3, 1] + sqr[3, 2] + sqr[3, 3])
    norm = jnp.sqrt(jnp.full((8, 128), squares, F32))
    norm_ref[...] = norm
    clip_ref[...] = jnp.minimum(1.0, 1.0 / (norm + 1e-06))
    clip = clip_ref[0:1, 0:1]

    for copy in loading:
        copy.wait()
    row = pl.multiple_of(c * 64, 64)
    gpad[pl.ds(row, 64), :] = grad[2][c, y, z].astype(F32)
    cross = []
    for i in range(3):
        w, m, v = (held[3 * i + k][...] for k in range(3))
        if i < 2:
            g = grad[i][c, y, z].astype(F32) * inverse
            piece[i][...] = adamw_update(w, m, v, g, clip)[0].astype(BF16)
            source = piece[i]
        else:
            g = gpad[0:118, :] * inverse
            piece[i][112:128, :] = jnp.zeros((16, 384), BF16)
            piece[i][0:118, :] = adamw_update(w, m, v, g, clip)[0].astype(BF16)
            source = piece[i].at[pl.ds(row, 64), :]
        cross.append(pair(source, other[i].at[c, y, z], xnb))

    over_y = []
    for i in range(3):
        for wait in wave_g[i]:
            wait.wait_recv()
        over_y.append(pair(grad[i].at[c, y], grad[i].at[c, y], ynb))
    wave_w = []
    for i in range(3):
        cross[i].wait_recv()
        wave_w.append(spread(lambda t: other[i].at[c, y, z], lambda t: other[i].at[c, y, t]))
    over_c = []
    for i in range(3):
        over_y[i].wait_recv()
        over_c.append(pair(grad[i].at[c], grad[i].at[c], sib))
    over_y = []
    for i in range(3):
        for wait in wave_w[i]:
            wait.wait_recv()
        over_y.append(pair(other[i].at[c, y], other[i].at[c, y], ynb))
    for i in range(3):
        over_y[i].wait_recv()
        over_c.append(pair(other[i].at[c], other[i].at[c], sib))
    for copy in over_c:
        copy.wait_recv()
    for copy in pending:
        copy.wait_send()


def run_exchange(reps, inverse, sums, states):
    half = tuple(jax.ShapeDtypeStruct((2, 2, 4, *p), BF16) for p in PIECES)
    tile = jax.ShapeDtypeStruct((8, 128), F32)
    held = [pltpu.VMEM(p, F32) for p in (PIECES[0], PIECES[1], (118, 384)) for _ in range(3)]
    scratch = [pltpu.VMEM((2, 2, 4, *p), BF16) for p in PIECES]
    scratch += [pltpu.VMEM((2, 4, *p), BF16) for p in PIECES]
    scratch += [pltpu.VMEM((4, *p), BF16) for p in PIECES]
    scratch += [pltpu.VMEM((4, *p), BF16) for p in PIECES]
    scratch += [pltpu.VMEM(p, BF16) for p in (PIECES[0], PIECES[1], (128, 384))]
    scratch += held
    scratch += [
        pltpu.VMEM((128, 384), F32),
        pltpu.VMEM((8, 128), F32),
        pltpu.VMEM((4, 4, 8, 128), F32),
        pltpu.SemaphoreType.DMA((9,)),
        pltpu.SemaphoreType.DMA((27,)),
        pltpu.SemaphoreType.DMA((27,)),
        pltpu.SemaphoreType.DMA((10, 3)),
        pltpu.SemaphoreType.DMA((10, 4)),
    ]
    return pl.pallas_call(
        functools.partial(exchange, reps, inverse),
        out_shape=half + half + (tile, tile),
        in_specs=[VMEM] * 3 + [HBM] * 9,
        out_specs=[VMEM] * 8,
        scratch_shapes=scratch,
        compiler_params=pltpu.CompilerParams(
            collective_id=0, has_side_effects=True, vmem_limit_bytes=LIMIT),
        name="exchange",
    )(*sums, *states)


def finish_rows(inverse, lead, clip_ref, g_ref, o_ref, w, m, v, nw, nm, nv, full):
    s = lax.axis_index("shard")
    clip = clip_ref[0:1, 0:1]
    new = adamw_update(w[...], m[...], v[...], g_ref[...].astype(F32) * inverse, clip)
    nw[...], nm[...], nv[...] = new
    if lead:
        full[0, s] = new[0][0].astype(BF16)
        full[0, 1 - s] = o_ref[0]
    else:
        full[s] = new[0].astype(BF16)
        full[1 - s] = o_ref[...]


def finish_chan(inverse, clip_ref, g_ref, o_ref, w, m, v, nw, nm, nv, full):
    s = lax.axis_index("shard")
    clip = clip_ref[0:1, 0:1]
    for c in range(2):
        rows = 64 if c == 0 else TAIL
        for z in range(4):
            at = (0, slice(c * 64, c * 64 + rows), slice(z * 384, z * 384 + 384))
            g = g_ref[c, 0, z, 0:rows].astype(F32) * inverse
            new = adamw_update(w[at], m[at], v[at], g, clip)
            nw[at], nm[at], nv[at] = new
            own = pl.multiple_of(s * 1536 + z * 384, 128)
            far = pl.multiple_of((1 - s) * 1536 + z * 384, 128)
            full[0, c * 64:c * 64 + rows, pl.ds(own, 384)] = new[0].astype(BF16)
            full[0, c * 64:c * 64 + rows, pl.ds(far, 384)] = o_ref[c, 0, z, 0:rows]


def finish(inverse, clip, grads, others, states):
    params = pltpu.CompilerParams(vmem_limit_bytes=LIMIT)
    tile = pl.BlockSpec((8, 128), lambda *i: (0, 0))
    results = []
    block = pl.BlockSpec((128, 1536), lambda i: (i, 0))
    state = jax.ShapeDtypeStruct((512, 1536), F32)
    results.append(pl.pallas_call(
        functools.partial(finish_rows, inverse, False),
        grid=(4,),
        in_specs=[tile] + [block] * 5,
        out_specs=[block] * 3 + [pl.BlockSpec((2, 128, 1536), lambda i: (0, i, 0))],
        out_shape=[state] * 3 + [jax.ShapeDtypeStruct((2, 512, 1536), BF16)],
        compiler_params=params, name="finish_embed",
    )(clip, grads[0].reshape(512, 1536), others[0].reshape(512, 1536), *states[0:3]))
    block = pl.BlockSpec((1, 768, 128), lambda l, i: (l, i, 0))
    state = jax.ShapeDtypeStruct((2, 1536, 128), F32)
    results.append(pl.pallas_call(
        functools.partial(finish_rows, inverse, True),
        grid=(2, 2),
        in_specs=[tile] + [block] * 5,
        out_specs=[block] * 3 + [pl.BlockSpec((1, 2, 768, 128), lambda l, i: (l, 0, i, 0))],
        out_shape=[state] * 3 + [jax.ShapeDtypeStruct((2, 2, 1536, 128), BF16)],
        compiler_params=params, name="finish_xproj",
    )(clip, grads[1].reshape(2, 1536, 128), others[1].reshape(2, 1536, 128), *states[3:6]))
    block = pl.BlockSpec((1, 118, 1536), lambda l: (l, 0, 0))
    part = pl.BlockSpec((2, 1, 4, 64, 384), lambda l: (0, l, 0, 0, 0))
    state = jax.ShapeDtypeStruct((2, 118, 1536), F32)
    results.append(pl.pallas_call(
        functools.partial(finish_chan, inverse),
        grid=(2,),
        in_specs=[tile, part, part] + [block] * 3,
        out_specs=[block] * 3 + [pl.BlockSpec((1, 118, 3072), lambda l: (l, 0, 0))],
        out_shape=[state] * 3 + [jax.ShapeDtypeStruct((2, 118, 3072), BF16)],
        compiler_params=params, name="finish_chan",
    )(clip, grads[2], others[2], *states[6:9]))
    return results


def on_device(gx, gc, ge, wx, wc, we, mx, mc, me, vx, vc, ve):
    reps, shards = lax.axis_size("rep"), lax.axis_size("shard")
    inverse = 1.0 / (gx.shape[0] * reps * shards)
    sums = local_sums(ge, gx, gc)
    extra = reps // 16
    if extra > 1:
        groups = [[z * (reps // 4) + y * (reps // 8) + e * 2 + c for e in range(extra)]
                  for z in range(4) for y in range(2) for c in range(2)]
        sums = [lax.psum(v.astype(F32), "rep", axis_index_groups=groups).astype(BF16)
                for v in sums]
    sums = [v.reshape(2, 2, 2, 4, *p) for v, p in zip(sums, PIECES)]
    states = (we, me, ve, wx, mx, vx, wc, mc, vc)
    out = run_exchange(reps, inverse, sums, states)
    norm, clip = out[6], out[7]
    (nwe, nme, nve, fe), (nwx, nmx, nvx, fx), (nwc, nmc, nvc, fc) = finish(
        inverse, clip, out[0:3], out[3:6], states)
    return (nwx, nwc, nwe, nmx, nmc, nme, nvx, nvc, nve,
            fx.reshape(2, 3072, 128), fc, fe.reshape(1024, 1536), norm[0, 0:1])


def solution(mesh):
    rows, cols, lead = P(None, "shard", None), P(None, None, "shard"), P("shard", None)
    spread = ("rep", "shard")
    return jax.shard_map(
        on_device,
        mesh=mesh,
        in_specs=(P(spread, None, None, None), P(spread, None, None, None),
                  P(spread, None, None)) + (rows, cols, lead) * 3,
        out_specs=(rows, cols, lead) * 3 + (P(), P(), P(), P()),
        check_vma=False,
    )
```

time: 559 us -> 178 us (0.32)
  local copies, waits for them, and re-layouts: 241 us -> 21.7 us
  Pallas kernels: 0 us -> 155 us
  blocking collectives: 142 us -> 0 us
  waiting for transfers between devices: 110 us -> 0 us
  other arithmetic: 43.6 us -> 0 us
  between operations: 18 us -> 0.69 us
    unnamed x13 -> x26, local copies, waits for them, and re-layouts: 241 us -> 21.2 us
    pallas_call x0 -> x7, Pallas kernels: none -> 155 us  [the longest x1 118 us: run_exchange(): pl.pallas_call(functools.partial(exchange, reps, inverse), out_shape=half...]
    psum x2 -> x0, blocking collectives: 142 us -> none  [the longest x1 138 us: on_device(): blocks = lax.psum((group[0], group[1], group[2]), 'rep')]
    all_gather x3 -> x0, waiting for transfers between devices: 90.2 us -> none  [the longest x1 47 us: on_device(): lax.all_gather(we.astype(jnp.bfloat16), 'shard', axis=0, tiled=True)]
    convert_element_type x3 -> x0, other arithmetic: 22.4 us -> none  [the longest x1 8.44 us: on_device(): wc.astype(jnp.bfloat16)]
    reduce_sum x6 -> x0, other arithmetic: 21.2 us -> none  [the longest x1 6.51 us: on_device(): summed_e = jnp.sum(grad_embed, axis=0, dtype=jnp.float32)]
    unnamed x7 -> x0, waiting for transfers between devices: 19.3 us -> none
  transfers between devices with their start and end apart: 6 -> 0, of which waited for: 4 -> 0; matrix products, arithmetic and copies ran while one was open for 18% -> 0% of each run, Pallas kernels for 0% -> 0%
where the time goes in v1:
time: 178 us; the launch traced here: 177 us
  Pallas kernels  155 us (87%)
  local copies, waits for them, and re-layouts  21.7 us (12%)
    pallas_call x1, Pallas kernels, run_exchange(): pl.pallas_call(functools.partial(exchange, reps, inverse), out_shape=half...  118 us
    unnamed x26, local copies, waits for them, and re-layouts  21.2 us
    pallas_call x1, Pallas kernels, finish(): pl.pallas_call(functools.partial(finish_rows, inverse, False), grid=(4,),...  10.6 us
    pallas_call x1, Pallas kernels, local_sums(): pl.pallas_call(sum_embed, grid=(8,), in_specs=[pl.BlockSpec((2, 128, 1536...  6.99 us
    pallas_call x1, Pallas kernels, finish(): pl.pallas_call(functools.partial(finish_rows, inverse, True), grid=(2, 2)...  6.24 us
    pallas_call x1, Pallas kernels, finish(): pl.pallas_call(functools.partial(finish_chan, inverse), grid=(2,), in_spe...  4.74 us
    pallas_call x1, Pallas kernels, local_sums(): pl.pallas_call(sum_xproj, grid=(2, 2), in_specs=[pl.BlockSpec((2, 1, 1536...  4 us
    pallas_call x1, Pallas kernels, local_sums(): pl.pallas_call(sum_chan, grid=(2, 2), in_specs=[pl.BlockSpec((2, 1, 118,...  3.97 us

profile of v1, /device:TPU:1, one launch (start us, length us, event | category | flops | bytes accessed | tf_op | source)
XLA Modules:
  0.0 177.3 jit_solution(11647508004556123889)
XLA Ops:
  0.6 0.0 copy-start.7
  0.7 2.9 %copy.26.refs_9_.w = f32[2,118,1536]{2,1,0:T(8,128)} copy(f32[2,118,1536]{2,0,1:T(2,128)} %param.16) | data formatting | bytes 2899968 | tf_op args[4]
  3.5 0.0 copy-done.7
  3.5 0.0 copy-start.8
  3.5 1.4 copy.27.refs_10_.m
  4.9 0.4 copy-done.8
  5.3 0.0 copy-start.3
  5.3 1.4 copy.28.refs_11_.v
  6.7 1.0 copy-done.3
  7.6 2.4 %copy.25.g_ref = bf16[2,2,118,3072]{3,2,1,0:T(8,128)(2,1)} copy(bf16[2,2,118,3072]{3,1,2,0:T(2,128)(2,1)S(1)} %copy-done.3) | data formatting | bytes 5799936 | tf_op args[1]
  10.0 4.0 %sum_chan.1.refs_2_ = bf16[2,2,2,4,64,384]{5,4,3,2,1,0:T(8,128)(2,1)} custom-call(bf16[2,2,118,3072]{3,2,1,0:T(8,128)(2,1)} %copy.25.g_ref), custom_call_target="tpu_custom_call" | custom-call | tf_op jit(solution)/shard_map/sum_chan/pallas_call | solution.py:74
  14.0 7.0 %sum_embed.1 = bf16[1024,1536]{1,0:T(8,128)(2,1)} custom-call(bf16[2,1024,1536]{2,1,0:T(8,128)(2,1)} %g_ref.3), custom_call_target="tpu_custom_call" | custom-call | tf_op jit(solution)/shard_map/sum_embed/pallas_call | solution.py:58
  20.9 4.0 %sum_xproj.1 = bf16[2,2,1536,128]{3,2,1,0:T(8,128)(2,1)} custom-call(bf16[2,2,3072,128]{3,2,1,0:T(8,128)(2,1)} %g_ref.4), custom_call_target="tpu_custom_call" | custom-call | tf_op jit(solution)/shard_map/sum_xproj/pallas_call | solution.py:66
  24.9 118.4 %exchange.1 = (bf16[2,2,4,32,1536]{4,3,2,1,0:T(8,128)(2,1)}, bf16[2,2,4,192,128]{4,3,2,1,0:T(8,128)(2,1)S(1)}, bf16[2,2,4,64,384]{4,3,2,1,0:T(8,128)(2,1)S(1)}, ...) custom-call(bf16[2,2,2,4,32,1536]{5,4,3,2,1,0:T(8,128)(2,1)} %bitcas, ...), custom_call_target="tpu_custom_call" | custom-call | tf_op jit(solution)/shard_map/exchange/pallas_call | solution.py:296
  143.3 0.0 copy-start.1
  143.3 1.1 copy-done.1
  144.5 4.7 %finish_chan.1 = (f32[2,118,1536]{2,1,0:T(8,128)}, f32[2,118,1536]{2,1,0:T(8,128)}, f32[2,118,1536]{2,1,0:T(8,128)}, bf16[2,118,3072]{2,1,0:T(8,128)(2,1)}) custom-call(f32[8,128]{1,0:T(8,128)S(1)} %get-tuple-element.33.clip_ref, bf16[2,2,4,64,384]{4,3,2,1,0:T(8,128)(2,1)S(1)} %get-tuple-element.37.g_ref, bf16[2,2,4,64,384]{4,3,2,1,0:T(8,128)(2,1)S(1)} %copy-done.1, ...), custom_call_target="tpu_custom_call" | custom-call | tf_op jit(solution)/shard_map/finish_chan/pallas_call | solution.py:364
  149.2 0.0 copy-start.6
  149.2 3.7 %copy.32 = f32[2,118,1536]{2,0,1:T(2,128)} copy(f32[2,118,1536]{2,1,0:T(8,128)} %get-tuple-element.54) | data formatting | bytes 2899968
  152.9 0.0 copy-start.5
  152.9 0.0 copy-done.6
  152.9 2.2 %copy.33 = f32[2,118,1536]{2,0,1:T(2,128)} copy(f32[2,118,1536]{2,1,0:T(8,128)S(1)} %copy-done.6) | data formatting | bytes 2899968
  155.1 0.0 copy-start.4
  155.1 0.0 copy-done.5
  155.1 2.2 %copy.34 = f32[2,118,1536]{2,0,1:T(2,128)} copy(f32[2,118,1536]{2,1,0:T(8,128)S(1)} %copy-done.5) | data formatting | bytes 2899968
  157.4 0.0 copy-start
  157.4 0.0 copy-done.4
  157.4 2.6 %copy.35 = bf16[2,118,3072]{2,0,1:T(2,128)(2,1)} copy(bf16[2,118,3072]{2,1,0:T(8,128)(2,1)S(1)} %copy-done.4) | data formatting | bytes 2899968
  160.0 0.0 copy-done
  160.0 0.0 copy-start.2
  160.0 10.6 %finish_embed.1 = (f32[512,1536]{1,0:T(8,128)}, f32[512,1536]{1,0:T(8,128)}, f32[512,1536]{1,0:T(8,128)}, bf16[2,512,1536]{2,1,0:T(8,128)(2,1)}) custom-call(f32[8,128]{1,0:T(8,128)S(1)} %get-tuple-element.33.clip_ref, bf16[512,1536]{1,0:T(8,128)(2,1)S(1)} %bitcast.9, bf16[512,1536]{1,0:T(8,128)(2,1)} %bitcast.14, f32[512,1536]{1,0:T(8,128)} %w.4, ...), custom_call_target="tpu_custom_call" | custom-call | tf_op jit(solution)/shard_map/finish_embed/pallas_call | solution.py:343
  170.6 0.0 copy-done.2
  170.6 6.2 %finish_xproj.1 = (f32[2,1536,128]{2,1,0:T(8,128)}, f32[2,1536,128]{2,1,0:T(8,128)}, f32[2,1536,128]{2,1,0:T(8,128)}, bf16[2,2,1536,128]{3,2,1,0:T(8,128)(2,1)}) custom-call(f32[8,128]{1,0:T(8,128)S(1)} %get-tuple-element.33.clip_ref, bf16[2,1536,128]{2,1,0:T(8,128)(2,1)S(1)} %bitcast.10, bf16[2,1536,128]{2,1,0:T(8,128)(2,1)S(1)} %bitcast.11, ...), custom_call_target="tpu_custom_call" | custom-call | tf_op jit(solution)/shard_map/finish_xproj/pallas_call | solution.py:353
  176.8 0.5 slice.3
Async XLA Ops:
  0.6 2.9 %copy-start.7 = (f32[2,118,1536]{2,0,1:T(2,128)S(1)}, f32[2,118,1536]{2,0,1:T(2,128)}, u32[]{:S(2)}) copy-start(f32[2,118,1536]{2,0,1:T(2,128)} %param.19) | copy-start | bytes 4349956
  3.5 1.7 copy-start.8
  5.3 2.4 %copy-start.3 = (bf16[2,2,118,3072]{3,1,2,0:T(2,128)(2,1)S(1)}, bf16[2,2,118,3072]{3,1,2,0:T(2,128)(2,1)}, u32[]{:S(2)}) copy-start(bf16[2,2,118,3072]{3,1,2,0:T(2,128)(2,1)} %param.13) | copy-start | bytes 8699908
  143.3 1.1 copy-start.1
  149.2 3.7 %copy-start.6 = (f32[2,118,1536]{2,1,0:T(8,128)S(1)}, f32[2,118,1536]{2,1,0:T(8,128)}, u32[]{:S(2)}) copy-start(f32[2,118,1536]{2,1,0:T(8,128)} %get-tuple-element.57) | copy-start | bytes 4349956
  152.9 2.2 %copy-start.5 = (f32[2,118,1536]{2,1,0:T(8,128)S(1)}, f32[2,118,1536]{2,1,0:T(8,128)}, u32[]{:S(2)}) copy-start(f32[2,118,1536]{2,1,0:T(8,128)} %get-tuple-element.60) | copy-start | bytes 4349956
  155.1 2.2 %copy-start.4 = (bf16[2,118,3072]{2,1,0:T(8,128)(2,1)S(1)}, bf16[2,118,3072]{2,1,0:T(8,128)(2,1)}, u32[]{:S(2)}) copy-start(bf16[2,118,3072]{2,1,0:T(8,128)(2,1)} %get-tuple-element.63) | copy-start | bytes 4349956
  157.4 2.6 %copy-start = (bf16[2,2,4,32,1536]{4,3,2,1,0:T(8,128)(2,1)S(1)}, bf16[2,2,4,32,1536]{4,3,2,1,0:T(8,128)(2,1)}, u32[]{:S(2)}) copy-start(bf16[2,2,4,32,1536]{4,3,2,1,0:T(8,128)(2,1)} %get-tuple-element.40) | copy-start | bytes 4718596
  160.0 10.6 %copy-start.2 = (bf16[2,2,4,192,128]{4,3,2,1,0:T(8,128)(2,1)S(1)}, bf16[2,2,4,192,128]{4,3,2,1,0:T(8,128)(2,1)}, u32[]{:S(2)}) copy-start(bf16[2,2,4,192,128]{4,3,2,1,0:T(8,128)(2,1)} %get-tuple-element.35) | copy-start | bytes 2359300

commit v2 on v1

v2 whole, which is shorter than its diff:
```python
import functools

import jax
import jax.numpy as jnp
from jax import lax
from jax.experimental import pallas as pl
from jax.experimental.pallas import tpu as pltpu
from jax.sharding import PartitionSpec as P

beta_one = 0.9
beta_two = 0.999
learn_rate = 0.003
decay_rate = 0.1
epsilon = 1e-08
correct_one = 0.9999734386011124
correct_two = 0.09520785288629094

F32 = jnp.float32
BF16 = jnp.bfloat16
MESH = pl.DeviceIdType.MESH
VMEM = pl.BlockSpec(memory_space=pltpu.VMEM)
HBM = pl.BlockSpec(memory_space=pl.ANY)
PIECES = ((32, 768), (32, 768), (192, 128), (64, 384))
TAIL = 54
LIMIT = 52 * 1024 * 1024


def adamw_update(weight, moment, second, gradient, clip_factor):
    clipped = clip_factor * gradient
    new_moment = beta_one * moment + (1.0 - beta_one) * clipped
    new_second = beta_two * second + (1.0 - beta_two) * clipped * clipped
    root = jnp.sqrt(new_second * (1.0 / correct_two)) + epsilon
    step_size = new_moment * (1.0 / correct_one) / root
    new_weight = weight - learn_rate * (step_size + decay_rate * weight)
    return (new_weight, new_moment, new_second)


def add_pair(first, second):
    return (first.astype(F32) + second.astype(F32)).astype(BF16)


def sum_kernel(e_ref, x_ref, left, right, x_out):
    left[...] = add_pair(e_ref[0, :, 0:768], e_ref[1, :, 0:768])
    right[...] = add_pair(e_ref[0, :, 768:1536], e_ref[1, :, 768:1536])
    x_out[0] = add_pair(x_ref[0], x_ref[1])


def sum_chan(g_ref, o_ref):
    for c in range(2):
        rows = 64 if c == 0 else TAIL
        for z in range(4):
            at = (0, slice(c * 64, c * 64 + rows), slice(z * 384, z * 384 + 384))
            total = g_ref[(0, *at)].astype(F32) + g_ref[(1, *at)].astype(F32)
            if rows < 64:
                o_ref[0, c, 0, z] = jnp.zeros((64, 384), BF16)
            o_ref[0, c, 0, z, 0:rows] = total.astype(BF16)


def local_sums(grad_e, grad_x, grad_c):
    half = jax.ShapeDtypeStruct((1024, 768), BF16)
    left, right, x = pl.pallas_call(
        sum_kernel,
        grid=(8,),
        in_specs=[pl.BlockSpec((2, 128, 1536), lambda i: (0, i, 0)),
                  pl.BlockSpec((2, 2, 384, 128), lambda i: (0, 0, i, 0))],
        out_specs=[pl.BlockSpec((128, 768), lambda i: (i, 0)),
                   pl.BlockSpec((128, 768), lambda i: (i, 0)),
                   pl.BlockSpec((1, 2, 384, 128), lambda i: (i // 4, 0, i % 4, 0))],
        out_shape=[half, half, jax.ShapeDtypeStruct((2, 2, 1536, 128), BF16)],
        name="local_sum",
    )(grad_e, grad_x)
    c = pl.pallas_call(
        sum_chan,
        grid=(2, 2),
        in_specs=[pl.BlockSpec((2, 1, 118, 1536), lambda s, y: (0, y, 0, s))],
        out_specs=pl.BlockSpec((1, 2, 1, 4, 64, 384), lambda s, y: (s, 0, y, 0, 0, 0)),
        out_shape=jax.ShapeDtypeStruct((2, 2, 2, 4, 64, 384), BF16),
        name="sum_chan",
    )(grad_c)
    return left, right, x, c


def exchange(reps, inverse, *refs):
    inp = refs[0:4]
    states = refs[4:13]
    grad = refs[13:17]
    other = refs[17:21]
    norm_ref, clip_ref = refs[21:23]
    bc, b2, b3, b4 = refs[23:27], refs[27:31], refs[31:35], refs[35:39]
    piece = refs[39:43]
    held = refs[43:55]
    gpad, sq, sqr, loads, pair_s, pair_r, many_s, many_r = refs[55:63]

    rep, s = lax.axis_index("rep"), lax.axis_index("shard")
    stride_z, stride_y = reps // 4, reps // 8
    c = lax.rem(rep, 2)
    y = lax.rem(rep // stride_y, 2)
    z = rep // stride_z
    sib = (rep + 1 - 2 * c, s)
    ynb = (rep + (1 - 2 * y) * stride_y, s)
    xnb = (rep, 1 - s)
    zs = [lax.rem(z + d, 4) for d in (1, 2, 3)]
    znb = [(rep + (t - z) * stride_z, s) for t in zs]

    barrier = pltpu.get_barrier_semaphore()
    for dev in (sib, ynb, xnb, *znb):
        pl.semaphore_signal(barrier, inc=1, device_id=dev, device_id_type=MESH)
    pl.semaphore_wait(barrier, 6)

    pending = []
    count = [0, 0]

    def pair(src, dst, dev):
        k = count[0]
        count[0] += 1
        copy = pltpu.make_async_remote_copy(
            src_ref=src, dst_ref=dst, send_sem=pair_s.at[k], recv_sem=pair_r.at[k],
            device_id=dev, device_id_type=MESH)
        copy.start()
        pending.append(copy)
        return copy

    def spread(source, slot):
        k = count[1]
        count[1] += 1
        waits = []
        for d, (t, dev) in enumerate(zip(zs, znb)):
            copy = pltpu.make_async_remote_copy(
                src_ref=source(t), dst_ref=slot(z), send_sem=many_s.at[k, d],
                recv_sem=many_r.at[k, z], device_id=dev, device_id_type=MESH)
            copy.start()
            pending.append(copy)
            waits.append(pltpu.make_async_remote_copy(
                src_ref=source(t), dst_ref=slot(t), send_sem=many_s.at[k, d],
                recv_sem=many_r.at[k, t], device_id=dev, device_id_type=MESH))
        return waits

    def add(into, at_into, of, at_of, n):
        def one(k, carry):
            a, b = at_into(k), at_of(k)
            into[a] = (into[a].astype(F32) + of[b].astype(F32)).astype(BF16)
            return carry
        lax.fori_loop(0, n, one, 0)

    first = [pair(inp[i].at[:, 1 - c], bc[i], sib) for i in range(4)]

    loading = []
    for k in range(3):
        row = pl.multiple_of(c * 256, 256)
        for h in range(2):
            loading.append(pltpu.make_async_copy(
                states[k].at[pl.ds(row, 256), pl.ds(h * 768, 768)],
                held[3 * h + k], loads.at[3 * h + k]))
        row = pl.multiple_of(y * 768, 768)
        loading.append(pltpu.make_async_copy(
            states[3 + k].at[c, pl.ds(row, 768), :], held[6 + k], loads.at[6 + k]))
        loading.append(pltpu.make_async_copy(states[6 + k].at[y], held[9 + k], loads.at[9 + k]))
    for copy in loading:
        copy.start()

    second = []
    for i in range(4):
        first[i].wait_recv()
        for half in (0, 1):
            if i < 2:
                keep = s if half else 1 - s
                add(bc[i], lambda k: (keep, k // 4, k % 4),
                    inp[i], lambda k: (keep, c, k // 4, k % 4), 8)
                if not half:
                    second.append(pair(bc[i].at[1 - s], b2[i], xnb))
            else:
                keep = y if half else 1 - y
                add(bc[i], lambda k: (k // 4, keep, k % 4),
                    inp[i], lambda k: (k // 4, c, keep, k % 4), 8)
                if not half:
                    second.append(pair(bc[i].at[:, 1 - y], b2[i], ynb))
    third = []
    for i in range(4):
        second[i].wait_recv()
        mine, dev = (y, ynb) if i < 2 else (s, xnb)
        for half in (0, 1):
            keep = mine if half else 1 - mine
            if i < 2:
                add(b2[i], lambda k: (keep, k), bc[i], lambda k: (s, keep, k), 4)
            else:
                add(b2[i], lambda k: (keep, k), bc[i], lambda k: (keep, y, k), 4)
            if not half:
                third.append(pair(b2[i].at[1 - mine], b3[i], dev))
    fourth = []
    for i in range(4):
        third[i].wait_recv()
        mine = y if i < 2 else s
        add(b3[i], lambda k: (k,), b2[i], lambda k: (mine, k), 4)
        fourth.append(spread(lambda t: b3[i].at[t], lambda t: b4[i].at[t]))

    sq[...] = jnp.zeros((8, 128), F32)
    gpad[...] = jnp.zeros((128, 384), F32)
    piece[3][:, 112:128, :] = jnp.zeros((4, 16, 384), BF16)
    wave_g = []
    for i in range(4):
        for wait in fourth[i]:
            wait.wait_recv()
        rows, cols = PIECES[i]
        total = b3[i][z].astype(F32)
        for t in zs:
            total = total + b4[i][t].astype(F32)
        grad[i][c, y, z] = total.astype(BF16)
        mean = total * inverse
        tile = (mean * mean).reshape(rows // 8, 8, cols).sum(axis=0)
        part = sq[...]
        for k in range(cols // 128):
            part = part + tile[:, k * 128:k * 128 + 128]
        sq[...] = part
        wave_g.append(spread(lambda t: grad[i].at[c, y, z], lambda t: grad[i].at[c, y, t]))

    for k, dev in enumerate((sib, xnb, ynb)):
        sqr[k, 0] = sq[...]
        pair(sqr.at[k, 0], sqr.at[k, 1], dev).wait_recv()
        sq[...] = sqr[k, 0] + sqr[k, 1]
    sqr[3, z] = sq[...]
    for wait in spread(lambda t: sqr.at[3, z], lambda t: sqr.at[3, t]):
        wait.wait_recv()
    squares = jnp.sum(sqr[3, 0] + sqr[3, 1] + sqr[3, 2] + sqr[3, 3])
    norm = jnp.sqrt(jnp.full((8, 128), squares, F32))
    norm_ref[...] = norm
    clip_ref[...] = jnp.minimum(1.0, 1.0 / (norm + 1e-06))
    clip = clip_ref[0:1, 0:1]

    for copy in loading:
        copy.wait()

    def update(i, at_y):
        rows = PIECES[i][0]

        def one(k, carry):
            first_row = (at_y * 4 + k) * rows if i < 2 else k * rows
            at = pl.ds(pl.multiple_of(first_row, rows), rows)
            w, m, v = (held[3 * i + q][at, :] for q in range(3))
            g = grad[i][c, at_y, k].astype(F32) * inverse
            new = adamw_update(w, m, v, g, clip)[0].astype(BF16)
            if i < 2:
                piece[i][at_y, k] = new
            else:
                piece[i][k] = new
            return carry

        def one_chan(k, carry):
            row, col = pl.multiple_of(c * 64, 64), pl.multiple_of(k * 384, 384)
            w, m, v = (held[9 + q][:, pl.ds(col, 384)] for q in range(3))
            gpad[pl.ds(row, 64), :] = grad[3][c, at_y, k].astype(F32) * inverse
            new = adamw_update(w, m, v, gpad[0:118, :], clip)[0]
            piece[3][k, 0:118, :] = new.astype(BF16)
            return carry

        lax.fori_loop(0, 4, one_chan if i == 3 else one, 0)
        if i == 3:
            source = piece[3].at[:, pl.ds(pl.multiple_of(c * 64, 64), 64), :]
            return pair(source, other[3].at[c, at_y], xnb)
        source = piece[i].at[at_y] if i < 2 else piece[i]
        return pair(source, other[i].at[c, at_y], xnb)

    over_y, cross, over_c = [], [], []
    for i in range(4):
        for wait in wave_g[i]:
            wait.wait_recv()
        over_y.append(pair(grad[i].at[c, y], grad[i].at[c, y], ynb))
        cross.append(update(i, y))
    cross_far = []
    for i in range(4):
        over_y[i].wait_recv()
        over_c.append(pair(grad[i].at[c], grad[i].at[c], sib))
        if i < 2:
            cross_far.append(update(i, 1 - y))
    over_y = []
    for i in (2, 3):
        cross[i].wait_recv()
        over_y.append(pair(other[i].at[c, y], other[i].at[c, y], ynb))
    for i in (0, 1):
        cross[i].wait_recv()
        cross_far[i].wait_recv()
        over_c.append(pair(other[i].at[c], other[i].at[c], sib))
    for i in (2, 3):
        over_y[i - 2].wait_recv()
        over_c.append(pair(other[i].at[c], other[i].at[c], sib))
    for copy in over_c:
        copy.wait_recv()
    for copy in pending:
        copy.wait_send()


def run_exchange(reps, inverse, sums, states):
    half = tuple(jax.ShapeDtypeStruct((2, 2, 4, *p), BF16) for p in PIECES)
    tile = jax.ShapeDtypeStruct((8, 128), F32)
    held = [pltpu.VMEM(p, F32) for p in ((256, 768), (256, 768), (768, 128), (118, 1536))
            for _ in range(3)]
    scratch = [pltpu.VMEM((2, 2, 4, *p), BF16) for p in PIECES]
    scratch += [pltpu.VMEM((2, 4, *p), BF16) for p in PIECES]
    scratch += [pltpu.VMEM((4, *p), BF16) for p in PIECES]
    scratch += [pltpu.VMEM((4, *p), BF16) for p in PIECES]
    scratch += [pltpu.VMEM(n, BF16) for n in (
        (2, 4, 32, 768), (2, 4, 32, 768), (4, 192, 128), (4, 128, 384))]
    scratch += held
    scratch += [
        pltpu.VMEM((128, 384), F32),
        pltpu.VMEM((8, 128), F32),
        pltpu.VMEM((4, 4, 8, 128), F32),
        pltpu.SemaphoreType.DMA((12,)),
        pltpu.SemaphoreType.DMA((40,)),
        pltpu.SemaphoreType.DMA((40,)),
        pltpu.SemaphoreType.DMA((10, 3)),
        pltpu.SemaphoreType.DMA((10, 4)),
    ]
    return pl.pallas_call(
        functools.partial(exchange, reps, inverse),
        out_shape=half + half + (tile, tile),
        in_specs=[VMEM] * 4 + [HBM] * 9,
        out_specs=[VMEM] * 10,
        scratch_shapes=scratch,
        compiler_params=pltpu.CompilerParams(
            collective_id=0, has_side_effects=True, vmem_limit_bytes=LIMIT),
        name="exchange",
    )(*sums, *states)


def finish_kernel(inverse, clip_ref, *refs):
    g, o, st = refs[0:4], refs[4:8], refs[8:17]
    out, full_e, full_x, full_c = refs[17:26], refs[26], refs[27], refs[28]
    s = lax.axis_index("shard")
    clip = clip_ref[0:1, 0:1]

    def step(k, at, grad):
        w, m, v = (st[k + q][at] for q in range(3))
        new = adamw_update(w, m, v, grad.astype(F32) * inverse, clip)
        for q in range(3):
            out[k + q][at] = new[q]
        return new[0].astype(BF16)

    for h in range(2):
        at = (slice(None), slice(h * 768, h * 768 + 768))
        full_e[(s, *at)] = step(0, at, g[h][...])
        full_e[(1 - s, *at)] = o[h][...]
    for layer in range(2):
        full_x[layer, s] = step(3, (layer,), g[2][layer])
        full_x[layer, 1 - s] = o[2][layer]
    for c in range(2):
        rows = 64 if c == 0 else TAIL
        at = (0, slice(c * 64, c * 64 + rows), slice(None))
        full_c[(s, *at)] = step(6, at, g[3][c, 0, 0, 0:rows])
        full_c[(1 - s, *at)] = o[3][c, 0, 0, 0:rows]


def finish(inverse, clip, grads, others, states):
    tile = pl.BlockSpec((8, 128), lambda i: (0, 0))
    half = pl.BlockSpec((64, 768), lambda i: (i, 0))
    e = pl.BlockSpec((64, 1536), lambda i: (i, 0))
    x = pl.BlockSpec((2, 192, 128), lambda i: (0, i, 0))
    c = pl.BlockSpec((1, 118, 384), lambda i: (i // 4, 0, i % 4))
    part = pl.BlockSpec((2, 1, 1, 64, 384), lambda i: (0, i // 4, i % 4, 0, 0))
    views = ((512, 768), (512, 768), (2, 1536, 128), (2, 2, 4, 64, 384))
    g = [v.reshape(n) for v, n in zip(grads, views)]
    o = [v.reshape(n) for v, n in zip(others, views)]
    shapes = ((512, 1536), (2, 1536, 128), (2, 118, 1536))
    out = pl.pallas_call(
        functools.partial(finish_kernel, inverse),
        grid=(8,),
        in_specs=[tile, half, half, x, part, half, half, x, part] + [e] * 3 + [x] * 3 + [c] * 3,
        out_specs=[e] * 3 + [x] * 3 + [c] * 3 + [
            pl.BlockSpec((2, 64, 1536), lambda i: (0, i, 0)),
            pl.BlockSpec((2, 2, 192, 128), lambda i: (0, 0, i, 0)),
            pl.BlockSpec((2, 1, 118, 384), lambda i: (0, i // 4, 0, i % 4))],
        out_shape=[jax.ShapeDtypeStruct(n, F32) for n in shapes for _ in range(3)] + [
            jax.ShapeDtypeStruct((2, 512, 1536), BF16),
            jax.ShapeDtypeStruct((2, 2, 1536, 128), BF16),
            jax.ShapeDtypeStruct((2, 2, 118, 1536), BF16)],
        compiler_params=pltpu.CompilerParams(vmem_limit_bytes=LIMIT),
        name="finish",
    )(clip, *g, *o, *states)
    full_c = out[11].transpose(1, 2, 0, 3).reshape(2, 118, 3072)
    return out, full_c


def on_device(gx, gc, ge, wx, wc, we, mx, mc, me, vx, vc, ve):
    reps, shards = lax.axis_size("rep"), lax.axis_size("shard")
    inverse = 1.0 / (gx.shape[0] * reps * shards)
    sums = local_sums(ge, gx, gc)
    extra = reps // 16
    if extra > 1:
        groups = [[z * (reps // 4) + y * (reps // 8) + e * 2 + c for e in range(extra)]
                  for z in range(4) for y in range(2) for c in range(2)]
        sums = [lax.psum(v.astype(F32), "rep", axis_index_groups=groups).astype(BF16)
                for v in sums]
    sums = [v.reshape(2, 2, 2, 4, *p) for v, p in zip(sums, PIECES)]
    states = (we, me, ve, wx, mx, vx, wc, mc, vc)
    out = run_exchange(reps, inverse, sums, states)
    norm, clip = out[8], out[9]
    new, full_c = finish(inverse, clip, out[0:4], out[4:8], states)
    nwe, nme, nve, nwx, nmx, nvx = new[0:6]
    nwc, nmc, nvc = new[6:9]
    return (nwx, nwc, nwe, nmx, nmc, nme, nvx, nvc, nve,
            new[10].reshape(2, 3072, 128), full_c, new[9].reshape(1024, 1536), norm[0, 0:1])


def solution(mesh):
    rows, cols, lead = P(None, "shard", None), P(None, None, "shard"), P("shard", None)
    spread = ("rep", "shard")
    return jax.shard_map(
        on_device,
        mesh=mesh,
        in_specs=(P(spread, None, None, None), P(spread, None, None, None),
                  P(spread, None, None)) + (rows, cols, lead) * 3,
        out_specs=(rows, cols, lead) * 3 + (P(), P(), P(), P()),
        check_vma=False,
    )
```

time: 178 us -> 160 us (0.90)
  Pallas kernels: 155 us -> 137 us
    pallas_call x1, Pallas kernels: 118 us -> 105 us  [run_exchange(): pl.pallas_call(functools.partial(exchange, reps, inverse), out_shape=half...]
    pallas_call x5 -> x2, Pallas kernels: 32.6 us -> 27.9 us  [the longest x1 20.1 us: finish(): pl.pallas_call(functools.partial(finish_kernel, inverse), grid=(8,), in_s...]
    unnamed x26 -> x21, local copies, waits for them, and re-layouts: 21.2 us -> 20.8 us
where the time goes in v2:
time: 160 us; the launch traced here: 159 us
  Pallas kernels  137 us (86%)
  local copies, waits for them, and re-layouts  21.3 us (13%)
    pallas_call x1, Pallas kernels, run_exchange(): pl.pallas_call(functools.partial(exchange, reps, inverse), out_shape=half...  105 us
    unnamed x21, local copies, waits for them, and re-layouts  20.8 us
    pallas_call x1, Pallas kernels, finish(): pl.pallas_call(functools.partial(finish_kernel, inverse), grid=(8,), in_s...  20.1 us
    pallas_call x1, Pallas kernels, local_sums(): pl.pallas_call(sum_kernel, grid=(8,), in_specs=[pl.BlockSpec((2, 128, 153...  7.85 us
    pallas_call x1, Pallas kernels, local_sums(): pl.pallas_call(sum_chan, grid=(2, 2), in_specs=[pl.BlockSpec((2, 1, 118,...  3.97 us

profile of v2, /device:TPU:1, one launch (start us, length us, event | category | flops | bytes accessed | tf_op | source)
XLA Modules:
  0.0 159.4 jit_solution(224142650731832428)
XLA Ops:
  0.6 0.0 copy-start.4
  0.7 2.9 %copy.36.refs_10_.refs_14_ = f32[2,118,1536]{2,1,0:T(8,128)} copy(f32[2,118,1536]{2,0,1:T(2,128)} %param.16) | data formatting | bytes 2899968 | tf_op args[4]
  3.6 0.0 copy-done.4
  3.6 0.0 copy-start.5
  3.6 1.4 copy.37.refs_11_.refs_15_
  4.9 0.4 copy-done.5
  5.3 0.0 copy-start
  5.3 1.4 copy.38.refs_12_.refs_16_
  6.7 1.0 copy-done
  7.7 2.4 %copy.35.g_ref = bf16[2,2,118,3072]{3,2,1,0:T(8,128)(2,1)} copy(bf16[2,2,118,3072]{3,1,2,0:T(2,128)(2,1)S(1)} %copy-done) | data formatting | bytes 5799936 | tf_op args[1]
  10.0 4.0 %sum_chan.1.refs_3_ = bf16[2,2,2,4,64,384]{5,4,3,2,1,0:T(8,128)(2,1)} custom-call(bf16[2,2,118,3072]{3,2,1,0:T(8,128)(2,1)} %copy.35.g_ref), custom_call_target="tpu_custom_call" | custom-call | tf_op jit(solution)/shard_map/sum_chan/pallas_call | solution.py:72
  14.0 7.9 %local_sum.1 = (bf16[1024,768]{1,0:T(8,128)(2,1)}, bf16[1024,768]{1,0:T(8,128)(2,1)}, bf16[2,2,1536,128]{3,2,1,0:T(8,128)(2,1)}) custom-call(bf16[2,1024,1536]{2,1,0:T(8,128)(2,1)} %e_ref.1, bf16[2,2,3072,128]{3,2,1,0:T(8,128)(2,1)} %x_ref.1), custom_call_target="tpu_custom_call" | custom-call | tf_op jit(solution)/shard_map/local_sum/pallas_call | solution.py:61
  21.8 105.5 %exchange.1 = (bf16[2,2,4,32,768]{4,3,2,1,0:T(8,128)(2,1)S(1)}, bf16[2,2,4,32,768]{4,3,2,1,0:T(8,128)(2,1)S(1)}, bf16[2,2,4,192,128]{4,3,2,1,0:T(8,128)(2,1)}, b...) custom-call(bf16[2,2,2,4,32,768]{5,4,3,2,1,0:T(8,128)(2,1)} %bitcast, ...), custom_call_target="tpu_custom_call" | custom-call | tf_op jit(solution)/shard_map/exchange/pallas_call | solution.py:313
  127.3 0.5 slice.3
  127.8 20.1 %finish.1 = (f32[512,1536]{1,0:T(8,128)}, f32[512,1536]{1,0:T(8,128)}, f32[512,1536]{1,0:T(8,128)}, f32[2,1536,128]{2,1,0:T(8,128)}, f32[2,1536,128]{2,1,0:T(8,1...) custom-call(f32[8,128]{1,0:T(8,128)S(1)} %get-tuple-element.41.clip_, ...), custom_call_target="tpu_custom_call" | custom-call | tf_op jit(solution)/shard_map/finish/pallas_call | solution.py:363
  147.9 0.0 copy-start.3
  147.9 3.7 %copy.43 = f32[2,118,1536]{2,0,1:T(2,128)} copy(f32[2,118,1536]{2,1,0:T(8,128)} %get-tuple-element.77) | data formatting | bytes 2899968
  151.6 0.0 copy-done.3
  151.6 0.0 copy-start.2
  151.6 2.2 %copy.44 = f32[2,118,1536]{2,0,1:T(2,128)} copy(f32[2,118,1536]{2,1,0:T(8,128)S(1)} %copy-done.3) | data formatting | bytes 2899968
  153.8 0.0 copy-done.2
  153.8 0.0 copy-start.1
  153.8 2.2 %copy.45 = f32[2,118,1536]{2,0,1:T(2,128)} copy(f32[2,118,1536]{2,1,0:T(8,128)S(1)} %copy-done.2) | data formatting | bytes 2899968
  156.1 0.0 copy-done.1
  156.1 1.5 copy.47
  157.5 1.8 %reshape.74 = bf16[2,118,3072]{2,0,1:T(2,128)(2,1)} reshape(bf16[2,118,2,1536]{3,2,0,1:T(2,128)(2,1)S(1)} %copy.47) | data formatting | bytes 2899968
Async XLA Ops:
  0.6 2.9 %copy-start.4 = (f32[2,118,1536]{2,0,1:T(2,128)S(1)}, f32[2,118,1536]{2,0,1:T(2,128)}, u32[]{:S(2)}) copy-start(f32[2,118,1536]{2,0,1:T(2,128)} %param.19) | copy-start | bytes 4349956
  3.6 1.7 %copy-start.5 = (f32[2,118,1536]{2,0,1:T(2,128)S(1)}, f32[2,118,1536]{2,0,1:T(2,128)}, u32[]{:S(2)}) copy-start(f32[2,118,1536]{2,0,1:T(2,128)} %param.22) | copy-start | bytes 4349956
  5.3 2.4 %copy-start = (bf16[2,2,118,3072]{3,1,2,0:T(2,128)(2,1)S(1)}, bf16[2,2,118,3072]{3,1,2,0:T(2,128)(2,1)}, u32[]{:S(2)}) copy-start(bf16[2,2,118,3072]{3,1,2,0:T(2,128)(2,1)} %param.13) | copy-start | bytes 8699908
  147.9 3.7 %copy-start.3 = (f32[2,118,1536]{2,1,0:T(8,128)S(1)}, f32[2,118,1536]{2,1,0:T(8,128)}, u32[]{:S(2)}) copy-start(f32[2,118,1536]{2,1,0:T(8,128)} %get-tuple-element.80) | copy-start | bytes 4349956
  151.6 2.2 %copy-start.2 = (f32[2,118,1536]{2,1,0:T(8,128)S(1)}, f32[2,118,1536]{2,1,0:T(8,128)}, u32[]{:S(2)}) copy-start(f32[2,118,1536]{2,1,0:T(8,128)} %get-tuple-element.83) | copy-start | bytes 4349956
  153.8 2.2 %copy-start.1 = (bf16[2,2,118,1536]{3,2,1,0:T(8,128)(2,1)S(1)}, bf16[2,2,118,1536]{3,2,1,0:T(8,128)(2,1)}, u32[]{:S(2)}) copy-start(bf16[2,2,118,1536]{3,2,1,0:T(8,128)(2,1)} %get-tuple-element.60) | copy-start | bytes 4349956
